TPU v7x, 32 devices: a whole 2x2x4 slice. The times are simulated.
32 devices in a mesh: dp: 8 (over z, y), mp: 4 (over x, core).
Axes of the slice: x: 2, y: 2, z: 4, core: 2. Of those that a mesh axis runs over, the one named last changes fastest.
Arguments:
- seg_queries: bfloat16 [8, 256, 3072], P('dp', None, 'mp'), may hold values from -6 to 6
- seg_keys: bfloat16 [8, 256, 3072], P('dp', None, 'mp'), may hold values from -6 to 6
- seg_values: bfloat16 [8, 256, 3072], P('dp', None, 'mp'), may hold values from -8 to 8
- memory_keys: bfloat16 [8, 256, 3072], P('dp', None, 'mp'), may hold values from -4 to 4
- memory_values: bfloat16 [8, 256, 3072], P('dp', None, 'mp'), may hold values from -8 to 8
- new_owner: int32 [8], replicated, may hold values from 0 to 7, each once
- kept_blocks: int32 [8], replicated, may hold values from 1 to 2, 12 in all
- rel_bias: float32 [24, 512], P('mp'), may hold values from -5 to 5
- norm_gain: float32 [3072], P('mp'), may hold values from 0.5 to 1.5
- cotangent: bfloat16 [8, 256, 3072], P('dp', None, 'mp'), may hold values from -8 to 8
Outputs:
- attended: bfloat16 [8, 256, 3072], P('dp', None, 'mp')
- query_grad: bfloat16 [8, 256, 3072], P('dp', None, 'mp')
- key_grad: bfloat16 [8, 256, 3072], P('dp', None, 'mp')
- value_grad: bfloat16 [8, 256, 3072], P('dp', None, 'mp')
- bias_grad: float32 [24, 512], P('mp', 'dp')
- gain_grad: float32 [3072], P('mp')
Inputs may be any that keep to these rules, and one draw needn't show every extreme that they name: `new_owner`: each old slot's stream goes to one device, and every device takes exactly one stream. A slot keeps its most recent kept_blocks blocks of 128 memory positions; some slot keeps all 2.
All inputs are finite; a program needn't handle non-finite values.
Results may differ from a plain program's by a relative error of at most 0.018.
Values may be sent and summed in bfloat16 or wider, within the bound.
A program may use at most 64 MiB of HBM per device.

v0:
```python
import jax
import jax.numpy as jnp
from jax import lax
from jax.sharding import PartitionSpec as P

DH = 128
BLOCK = 128
HD = 3072


def spread_table(bias_table, seg_len, pos_len):
    heads_here = bias_table.shape[0]
    full_width = pos_len + seg_len + 1
    padded = jnp.pad(bias_table, ((0, 0), (seg_len, 1)))
    tiled = jnp.tile(padded, (1, seg_len))[:, : seg_len * (full_width - 1)]
    skewed = tiled.reshape(heads_here, seg_len, full_width - 1)[:, :, seg_len : seg_len + pos_len]
    return skewed[:, ::-1, ::-1]


def diagonal_sums(score_grad, seg_len, pos_len):
    heads_here = score_grad.shape[0]
    flipped = score_grad[:, ::-1, ::-1]
    padded = jnp.pad(flipped, ((0, 0), (0, 0), (0, seg_len))).reshape(
        heads_here, seg_len * (pos_len + seg_len)
    )
    padded = jnp.pad(padded, ((0, 0), (0, seg_len))).reshape(
        heads_here, seg_len, pos_len + seg_len + 1
    )
    return jnp.sum(padded[:, :, :pos_len], axis=1)


def body(
    seg_queries,
    seg_keys,
    seg_values,
    memory_keys,
    memory_values,
    new_owner,
    kept_blocks,
    rel_bias,
    norm_gain,
    cotangent,
):
    own_index = lax.axis_index("dp")
    slot_count = lax.axis_size("dp")
    slot_ids = jnp.arange(slot_count, dtype=jnp.int32)
    matches = (new_owner[None, :] == slot_ids[:, None]).astype(jnp.int32)
    source = jnp.sum(matches * slot_ids[None, :], axis=1)
    kept_here = jnp.sum(jnp.where(new_owner == own_index, kept_blocks, 0))
    spread = (
        lax.all_to_all(memory_keys, "dp", split_axis=1, concat_axis=0, tiled=True),
        lax.all_to_all(memory_values, "dp", split_axis=1, concat_axis=0, tiled=True),
    )
    ordered = (jnp.take(spread[0], source, axis=0), jnp.take(spread[1], source, axis=0))
    mem_keys, mem_values = (
        lax.all_to_all(ordered[0], "dp", split_axis=0, concat_axis=1, tiled=True),
        lax.all_to_all(ordered[1], "dp", split_axis=0, concat_axis=1, tiled=True),
    )
    seg_len = seg_queries.shape[1]
    mem_len = mem_keys.shape[1]
    pos_len = mem_len + seg_len
    heads_here = rel_bias.shape[0]
    score_scale = DH ** (-0.5)
    query_heads = seg_queries[0].reshape(seg_len, heads_here, DH)
    key_heads = jnp.concatenate([mem_keys[0], seg_keys[0]], axis=0).reshape(pos_len, heads_here, DH)
    value_heads = jnp.concatenate([mem_values[0], seg_values[0]], axis=0).reshape(
        pos_len, heads_here, DH
    )
    query_pos = jnp.arange(seg_len, dtype=jnp.int32)[:, None]
    key_pos = jnp.arange(pos_len, dtype=jnp.int32)[None, :]
    allowed = (key_pos <= mem_len + query_pos) & (key_pos >= mem_len - BLOCK * kept_here)
    scores = (
        jnp.einsum("ihd,jhd->hij", query_heads, key_heads, preferred_element_type=jnp.float32)
        * score_scale
    )
    scores = scores + spread_table(rel_bias, seg_len, pos_len)
    row_max = jnp.max(jnp.where(allowed, scores, -1e30), axis=-1, keepdims=True)
    unnormed = jnp.where(allowed, jnp.exp(scores - row_max), 0.0)
    weights_f = unnormed / jnp.sum(unnormed, axis=-1, keepdims=True)
    weights_b = weights_f.astype(jnp.bfloat16)
    out_heads = jnp.einsum(
        "hij,jhd->ihd", weights_b, value_heads, preferred_element_type=jnp.float32
    )
    attn_out = out_heads.reshape(seg_len, heads_here * DH)
    square_total = lax.psum(jnp.sum(attn_out * attn_out, axis=1), "mp")
    inv_rms = lax.rsqrt(square_total / HD + 1e-06)
    attended = (attn_out * inv_rms[:, None] * norm_gain).astype(jnp.bfloat16)
    upstream = cotangent[0].astype(jnp.float32)
    gain_cot = upstream * norm_gain
    cross_sum = lax.psum(jnp.sum(gain_cot * attn_out, axis=1), "mp")
    out_grad = (
        inv_rms[:, None] * gain_cot - attn_out * (inv_rms**3 * cross_sum / HD)[:, None]
    ).astype(jnp.bfloat16)
    grad_heads = out_grad.reshape(seg_len, heads_here, DH)
    row_delta = jnp.einsum("ihd,ihd->hi", grad_heads.astype(jnp.float32), out_heads)
    prob_grad = jnp.einsum(
        "ihd,jhd->hij", grad_heads, value_heads, preferred_element_type=jnp.float32
    )
    score_grad = weights_f * (prob_grad - row_delta[:, :, None])
    score_grad_b = score_grad.astype(jnp.bfloat16)
    query_grad = (
        jnp.einsum("hij,jhd->ihd", score_grad_b, key_heads, preferred_element_type=jnp.float32)
        * score_scale
    )
    key_grad = (
        jnp.einsum(
            "hij,ihd->jhd",
            score_grad_b[:, :, mem_len:],
            query_heads,
            preferred_element_type=jnp.float32,
        )
        * score_scale
    )
    value_grad = jnp.einsum(
        "hij,ihd->jhd", weights_b[:, :, mem_len:], grad_heads, preferred_element_type=jnp.float32
    )
    local_bias = diagonal_sums(score_grad, seg_len, pos_len)
    local_gain = jnp.sum(upstream * attn_out * inv_rms[:, None], axis=0)
    bias_grad = lax.psum_scatter(local_bias, "dp", scatter_dimension=1, tiled=True)
    gain_grad = lax.psum(local_gain, "dp")
    row_shape = (1, seg_len, heads_here * DH)
    return (
        attended.reshape(row_shape),
        query_grad.reshape(row_shape).astype(jnp.bfloat16),
        key_grad.reshape(row_shape).astype(jnp.bfloat16),
        value_grad.reshape(row_shape).astype(jnp.bfloat16),
        bias_grad,
        gain_grad,
    )


def solution(mesh):
    in_specs = (
        P("dp", None, "mp"),
        P("dp", None, "mp"),
        P("dp", None, "mp"),
        P("dp", None, "mp"),
        P("dp", None, "mp"),
        P(),
        P(),
        P("mp", None),
        P("mp"),
        P("dp", None, "mp"),
    )
    out_specs = (
        P("dp", None, "mp"),
        P("dp", None, "mp"),
        P("dp", None, "mp"),
        P("dp", None, "mp"),
        P("mp", "dp"),
        P("mp"),
    )
    return jax.shard_map(body, mesh=mesh, in_specs=in_specs, out_specs=out_specs, check_vma=False)
```

profile of v0, /device:TPU:0, one launch (start us, length us, event | category | flops | bytes accessed | tf_op | source)
XLA Modules:
  0.0 278.5 jit_solution(3035780389378918912)
XLA Ops:
  7.2 1.7 copy.155
  8.8 0.5 broadcast.146
  9.3 3.0 %reduce.5 = bf16[256,768]{1,0:T(8,128)(2,1)S(1)} reduce(bf16[256,1,768]{2,1,0:T(2,128)(2,1)S(1)} %bitcast.75, bf16[]{:T(256)} %broadcast.146), dimensions={1}, to_apply=%bitcast.68.reduce_sub_computation | reduce | bytes 786434
  12.4 0.8 reshape.233
  13.2 7.3 %all-to-all-start = ((bf16[8,2,12288]{2,1,0:T(2,128)(2,1)}), bf16[8,2,12288]{2,1,0:T(2,128)(2,1)S(1)}, u32[]{:S(2)}, u32[]{:S(2)}) async-start(bf16[8,2,12288]{2,1,0:T(2,128)(2,1)} %reshape.233), calls=%async_computation | async-start | bytes 786432 | tf_op jit(solution)/shard_map/all_to_all | solution.py:52
  20.5 0.6 copy.154
  21.1 3.0 %reduce.6 = bf16[256,768]{1,0:T(8,128)(2,1)S(1)} reduce(bf16[256,1,768]{2,1,0:T(2,128)(2,1)S(1)} %bitcast.76, bf16[]{:T(256)} %broadcast.146), dimensions={1}, to_apply=%bitcast.67.reduce_sub_computation | reduce | bytes 786434
  24.1 0.8 reshape.231
  25.0 7.2 %all-to-all-done = bf16[8,2,12288]{2,1,0:T(2,128)(2,1)S(1)} async-done(((bf16[8,2,12288]{2,1,0:T(2,128)(2,1)}), bf16[8,2,12288]{2,1,0:T(2,128)(2,1)S(1)}, u32[]{:S(2)}, u32[]{:S(2)}) %all-to-all-start) | async-done | bytes 393248 | tf_op jit(solution)/shard_map/all_to_all | solution.py:52
  32.2 3.6 %all-to-all-start.2 = ((bf16[8,2,12288]{2,1,0:T(2,128)(2,1)}), bf16[8,2,12288]{2,1,0:T(2,128)(2,1)S(1)}, u32[]{:S(2)}, u32[]{:S(2)}) async-start(bf16[8,2,12288]{2,1,0:T(2,128)(2,1)} %reshape.231), calls=%async_computation.2 | async-start | bytes 786432 | tf_op jit(solution)/shard_map/all_to_all | solution.py:51
  36.0 0.4 reshape.234
  36.4 11.0 %all-to-all-done.2 = bf16[8,2,12288]{2,1,0:T(2,128)(2,1)S(1)} async-done(((bf16[8,2,12288]{2,1,0:T(2,128)(2,1)}), bf16[8,2,12288]{2,1,0:T(2,128)(2,1)S(1)}, u32[]{:S(2)}, u32[]{:S(2)}) %all-to-all-start.2) | async-done | bytes 393248 | tf_op jit(solution)/shard_map/all_to_all | solution.py:51
  47.8 0.6 gather_fusion
  48.4 0.6 gather_fusion.1
  49.0 0.9 broadcast_select_fusion.1
  49.9 14.9 %all_to_all.42 = bf16[8,32,768]{2,1,0:T(8,128)(2,1)S(1)} all-to-all(bf16[8,32,768]{2,1,0:T(8,128)(2,1)S(1)} %get-tuple-element.42), channel_id=1, replica_groups=mesh['dp'=8,'mp'=4] {'dp'}, dimensions={0} | all-to-all | bytes 786432 | tf_op jit(solution)/shard_map/all_to_all | solution.py:56
  64.8 4.1 %all-to-all-start.1 = ((bf16[8,32,768]{2,1,0:T(8,128)(2,1)}), bf16[8,32,768]{2,1,0:T(8,128)(2,1)}, u32[]{:S(2)}, u32[]{:S(2)}) async-start(bf16[8,32,768]{2,1,0:T(8,128)(2,1)} %get-tuple-element.41), calls=%async_computation.1 | async-start | bytes 786432 | tf_op jit(solution)/shard_map/all_to_all | solution.py:57
  69.2 2.8 %tile.4 = f32[6,256,769]{2,1,0:T(8,128)} broadcast(f32[6,769]{1,0:T(8,128)S(1)} %pad.12), dimensions={0,2} | broadcast | bytes 4743192 | tf_op jit(solution)/shard_map/tile | solution.py:15
  72.0 9.3 %tile.10 = f32[6,196864]{1,0:T(8,128)} reshape(f32[6,256,769]{2,1,0:T(8,128)} %tile.4) | data formatting | bytes 9449472 | tf_op jit(solution)/shard_map/tile | solution.py:15
  81.4 2.8 slice-done
  84.1 1.5 copy.153
  86.1 2.4 copy.146
  88.4 22.3 %rev.6 = f32[6,256,512]{1,2,0:T(8,128)S(1)} reverse(f32[6,256,512]{1,2,0:T(8,128)} %copy.146), dimensions={1,2} | reverse | bytes 6291456 | tf_op jit(solution)/shard_map/rev | solution.py:17
  110.8 1.9 copy.109
  112.7 1.9 copy.106
  114.6 1.9 copy.108
  116.5 1.9 copy.103
  118.4 2.0 copy.114
  120.5 0.6 fusion.22
  121.8 0.8 fusion.18
  122.6 1.3 concatenate.19
  123.8 1.1 copy.107
  124.9 2.2 concatenate.16
  127.2 2.0 copy.104
  129.2 1.7 bitcast_add_fusion
  130.9 1.2 fusion.29
  132.5 1.1 copy-done.1
  133.6 1.9 fusion.14
  135.5 5.8 %psum.21 = f32[256]{0:T(256)S(1)} all-reduce(f32[256]{0:T(256)} %get-tuple-element.45), channel_id=1, replica_groups=mesh['dp'=8,'mp'=4] {'mp'}, use_global_device_ids=true, to_apply=%region_5.7 | all-reduce | flops 256 | bytes 2048 | tf_op jit(solution)/shard_map/psum | solution.py:85
  141.3 0.6 copy-done.16
  141.9 2.2 fusion.13
  144.1 7.5 %psum.22 = f32[256]{0:T(256)} all-reduce(f32[256]{0:T(256)} %get-tuple-element.38), channel_id=1, replica_groups=mesh['dp'=8,'mp'=4] {'mp'}, use_global_device_ids=true, to_apply=%region_7.9 | all-reduce | flops 256 | bytes 2048 | tf_op jit(solution)/shard_map/psum | solution.py:90
  151.6 0.7 fusion.21
  152.3 1.6 fusion.11
  153.9 3.6 %fusion.30 = (bf16[6,256,512]{1,2,0:T(8,128)(2,1)S(1)}, f32[6,256,512]{1,2,0:T(8,128)}) fusion(f32[6,256]{1,0:T(8,128)S(1)} %get-tuple-element.39, bf16[256,6,128]{0,2,1:T(8,128)(2,1)S(1)} %get-tuple-element.40, bf16[256,6,128]{0,2,1:T(8,128)(2,1)} %bitcast.86, bf16[256,6,128]{0,2,1:T(8,128)(2,1)} %copy.104, f32[6,256,512]{1,2,0:T(8,128)S(1)} %get-tuple-element.44, ...), kind=kOutput, calls=%fused_computation.61 | convolution fusion | flops 206045184 | bytes 9056256 | tf_op jit(solution)/shard_map/ihd,jhd->hij/dot_general | solution.py:96
  157.5 1.2 fusion.7
  158.7 1.1 fusion.8
  159.8 0.4 convolution_convert_fusion
  160.2 1.2 copy.113
  161.4 22.3 %rev.7 = f32[6,256,512]{1,2,0:T(8,128)S(1)} reverse(f32[6,256,512]{1,2,0:T(8,128)} %get-tuple-element.48), dimensions={1,2} | reverse | bytes 6291456 | tf_op jit(solution)/shard_map/rev | solution.py:22
  183.8 2.4 copy.147
  186.1 2.3 pad_bitcast_fusion
  188.4 2.8 %copy.149 = f32[1,6,256,768]{3,1,2,0:T(8,128)S(1)} copy(f32[1,6,256,768]{3,2,1,0:T(8,128)S(1)} %pad_bitcast_fusion) | data formatting | bytes 9437184
  191.3 2.9 %pad.14 = f32[6,196864]{1,0:T(8,128)} pad(f32[6,196608]{1,0:T(8,128)S(1)} %bitcast.70, f32[]{:T(128)} %constant.16.clone.1), padding=0_0x0_256 | pad | bytes 9443332 | tf_op jit(solution)/shard_map/jit(_pad)/pad | solution.py:26
  194.2 10.5 %reshape.202 = f32[6,256,769]{2,1,0:T(8,128)} reshape(f32[6,196864]{1,0:T(8,128)} %pad.14) | data formatting | bytes 9449472 | tf_op jit(solution)/shard_map/reshape | solution.py:26
  204.7 2.3 slice_reduce_fusion
  207.1 0.8 copy.142
  207.9 0.9 multiply_convert_fusion
  208.8 0.9 copy.123
  209.8 0.9 copy.124
  210.7 0.9 copy.125
  211.6 22.1 %psum.23 = f32[768]{0:T(1024)} all-reduce(f32[768]{0:T(1024)S(1)} %bitcast.93), channel_id=1, replica_groups=mesh['dp'=8,'mp'=4] {'dp'}, use_global_device_ids=true, to_apply=%region_11.13 | all-reduce | flops 768 | bytes 6144 | tf_op jit(solution)/shard_map/psum | solution.py:120
  233.7 36.5 %reduce-scatter.4.cloned.1.call-done = f32[64,6]{1,0:T(8,128)} async-done(((f32[512,6]{1,0:T(8,128)}), f32[64,6]{1,0:T(8,128)}) %reduce-scatter.4.cloned.1.call-update) | async-done | bytes 1552
  270.2 1.4 copy.143
  (53 shorter events, 1.6 us)
Async XLA Ops:
  7.2 13.3 %copy-start.11 = (bf16[1,256,768]{2,1,0:T(8,128)(2,1)S(1)}, bf16[1,256,768]{2,1,0:T(8,128)(2,1)}, u32[]{:S(2)}) copy-start(bf16[1,256,768]{2,1,0:T(8,128)(2,1)} %param.15) | copy-start | bytes 1179652
  9.3 26.5 %copy-start.17 = (s32[8]{0:T(128)S(1)}, s32[8]{0:T(128)}, u32[]{:S(2)}) copy-start(s32[8]{0:T(128)} %param.17) | copy-start | bytes 100
  13.2 19.0 %all-to-all-start = ((bf16[8,2,12288]{2,1,0:T(2,128)(2,1)}), bf16[8,2,12288]{2,1,0:T(2,128)(2,1)S(1)}, u32[]{:S(2)}, u32[]{:S(2)}) async-start(bf16[8,2,12288]{2,1,0:T(2,128)(2,1)} %reshape.233), calls=%async_computation | async-start | bytes 786432 | tf_op jit(solution)/shard_map/all_to_all | solution.py:52
  32.2 15.2 %all-to-all-start.2 = ((bf16[8,2,12288]{2,1,0:T(2,128)(2,1)}), bf16[8,2,12288]{2,1,0:T(2,128)(2,1)S(1)}, u32[]{:S(2)}, u32[]{:S(2)}) async-start(bf16[8,2,12288]{2,1,0:T(2,128)(2,1)} %reshape.231), calls=%async_computation.2 | async-start | bytes 786432 | tf_op jit(solution)/shard_map/all_to_all | solution.py:51
  47.8 21.4 %copy-start.13 = (f32[6,512]{1,0:T(8,128)S(1)}, f32[6,512]{1,0:T(8,128)}, u32[]{:S(2)}) copy-start(f32[6,512]{1,0:T(8,128)} %param.19) | copy-start | bytes 36868
  64.8 60.1 %all-to-all-start.1 = ((bf16[8,32,768]{2,1,0:T(8,128)(2,1)}), bf16[8,32,768]{2,1,0:T(8,128)(2,1)}, u32[]{:S(2)}, u32[]{:S(2)}) async-start(bf16[8,32,768]{2,1,0:T(8,128)(2,1)} %get-tuple-element.41), calls=%async_computation.1 | async-start | bytes 786432 | tf_op jit(solution)/shard_map/all_to_all | solution.py:57
  68.9 201.3 %reduce-scatter.4.cloned.1.call-start = ((), (), s32[]{:S(2)}) async-start(), calls=%async_computation.5 | async-start | bytes 294912
  81.4 2.8 %slice-start = ((f32[6,196864]{1,0:T(8,128)}), f32[6,196608]{1,0:T(8,128)S(1)}, s32[]{:S(2)}) async-start(f32[6,196864]{1,0:T(8,128)} %tile.10), calls=%async_computation.6 | async-start | bytes 12582912 | tf_op jit(solution)/shard_map/slice | solution.py:15
  110.8 9.7 %copy-start.18 = (s32[8]{0:T(128)S(1)}, s32[8]{0:T(128)}, u32[]{:S(2)}) copy-start(s32[8]{0:T(128)} %param.18) | copy-start | bytes 100
  129.2 1.7 copy-start.6
  132.2 1.4 copy-start.7
  132.2 1.4 copy-start.8
  132.2 9.6 %copy-start.12 = (f32[768]{0:T(1024)S(1)}, f32[768]{0:T(1024)}, u32[]{:S(2)}) copy-start(f32[768]{0:T(1024)} %param.20) | copy-start | bytes 9220
  132.5 1.1 copy-start.1
  141.3 0.6 copy-start.16
  141.3 0.6 copy-start.14
  153.9 3.6 %copy-start.5 = (bf16[256,6,128]{2,0,1:T(8,128)(2,1)S(1)}, bf16[256,6,128]{2,0,1:T(8,128)(2,1)}, u32[]{:S(2)}) copy-start(bf16[256,6,128]{2,0,1:T(8,128)(2,1)} %copy.108) | copy-start | bytes 1179652
  153.9 4.8 %copy-start.4 = (bf16[1,256,768]{1,2,0:T(8,128)(2,1)S(1)}, bf16[1,256,768]{1,2,0:T(8,128)(2,1)}, u32[]{:S(2)}) copy-start(bf16[1,256,768]{1,2,0:T(8,128)(2,1)} %copy.109) | copy-start | bytes 1179652
  157.5 2.4 copy-start.2
  157.5 2.8 copy-start
  204.7 3.2 %copy-start.3 = (f32[1,256,768]{2,1,0:T(8,128)S(1)}, f32[1,256,768]{2,1,0:T(8,128)}, u32[]{:S(2)}) copy-start(f32[1,256,768]{2,1,0:T(8,128)} %copy.113) | copy-start | bytes 2359300
  204.7 3.2 %copy-start.15 = (f32[256]{0:T(256)S(1)}, f32[256]{0:T(256)}, u32[]{:S(2)}) copy-start(f32[256]{0:T(256)} %copy-done.14) | copy-start | bytes 3076
  204.7 4.1 %copy-start.9 = (bf16[6,128,256]{2,1,0:T(8,128)(2,1)S(1)}, bf16[6,128,256]{2,1,0:T(8,128)(2,1)}, u32[]{:S(2)}) copy-start(bf16[6,128,256]{2,1,0:T(8,128)(2,1)} %fusion.7) | copy-start | bytes 1179652
  204.7 5.0 %copy-start.10 = (bf16[6,256,128]{1,2,0:T(8,128)(2,1)S(1)}, bf16[6,256,128]{1,2,0:T(8,128)(2,1)}, u32[]{:S(2)}) copy-start(bf16[6,256,128]{1,2,0:T(8,128)(2,1)} %fusion.8) | copy-start | bytes 1179652
Sparse Core Ops, SparseCore 0:
  208.1 62.0 reduce-scatter.3
where the time goes:
time: 282 us; the launch traced here: 278 us
  local copies, waits for them, and re-layouts  116 us (41%)
  waiting for transfers between devices  54.7 us (19%)
  blocking collectives  50.3 us (18%)
  other arithmetic  17.7 us (6%)
  starting transfers between devices  15.2 us (5%)
  between operations  15 us (5%)
  matrix products  9.88 us (4%)
    unnamed x2, waiting for transfers between devices  36.5 us
    unnamed x60, local copies, waits for them, and re-layouts  29.3 us
    rev x1, local copies, waits for them, and re-layouts, spread_table(): return skewed[:, ::-1, ::-1]  22.3 us
    rev x1, local copies, waits for them, and re-layouts, diagonal_sums(): flipped = score_grad[:, ::-1, ::-1]  22.3 us
    psum x1, blocking collectives, body(): gain_grad = lax.psum(local_gain, 'dp')  22.1 us
    all_to_all x1, blocking collectives, body(): lax.all_to_all(ordered[0], 'dp', split_axis=0, concat_axis=1, tiled=True)  14.9 us
    another operation x2, local copies, waits for them, and re-layouts, spread_table(): tiled = jnp.tile(padded, (1, seg_len))[:, :seg_len * (full_width - 1)]  12.2 us
    all_to_all x1, waiting for transfers between devices, body(): lax.all_to_all(memory_keys, 'dp', split_axis=1, concat_axis=0, tiled=True)  11 us
  transfers between devices with their start and end apart: 4, of which 3 were waited for; matrix products, arithmetic and copies ran while one was open for 22% of the time, Pallas kernels for 0%

commit v1 on v0

v1 whole, which is shorter than its diff:
```python
import functools

import jax
import jax.numpy as jnp
from jax import lax
from jax.experimental import pallas as pl
from jax.experimental.pallas import tpu as pltpu
from jax.sharding import PartitionSpec as P

DH = 128
BLOCK = 128
HD = 3072
LANES = 128
MESH = pl.DeviceIdType.MESH
HIGHEST = lax.Precision.HIGHEST


def share_plan(n, mem_len, cols):
    col_groups = 1
    while n // col_groups > mem_len // 16 and col_groups < 2:
        col_groups *= 2
    members = min(n, (mem_len // 16) * col_groups)
    rows = mem_len // (members // col_groups)
    return members, rows, cols // col_groups, col_groups


def kernel(
    n,
    n_mp,
    plan,
    owner_ref,
    kept_ref,
    q_ref,
    k_ref,
    v_ref,
    mk_hbm,
    mv_hbm,
    bias_ref,
    gain_ref,
    cot_ref,
    att_ref,
    dq_ref,
    dk_ref,
    dv_ref,
    dbias_ref,
    dgain_ref,
    rx_k,
    rx_v,
    st_k,
    st_v,
    mem_k,
    mem_v,
    src_sm,
    prob,
    attn,
    mp_send,
    mp_recv,
    folded,
    diag,
    pkt,
    pkt_recv,
    p1_send,
    p1_recv,
    p2_send,
    p2_recv,
    mp_ssem,
    mp_rsem,
    dp_ssem,
    dp_rsem,
):
    members, rows, width, col_groups = plan
    me = lax.axis_index("dp")
    me_mp = lax.axis_index("mp")
    seg_len, cols = q_ref.shape
    mem_len = mem_k.shape[0]
    pos_len = mem_len + seg_len
    heads = cols // DH
    scale = DH ** (-0.5)
    every = members == n

    barrier = pltpu.get_barrier_semaphore()

    @pl.loop(1, n)
    def _(j):
        pl.semaphore_signal(
            barrier, inc=1, device_id={"dp": lax.rem(me + j, n)}, device_id_type=MESH
        )

    @pl.loop(1, n_mp)
    def _(j):
        pl.semaphore_signal(
            barrier, inc=1, device_id={"mp": lax.rem(me_mp + j, n_mp)}, device_id_type=MESH
        )

    pl.semaphore_wait(barrier, n - 1 + n_mp - 1)

    def guard(condition, run):
        if every:
            run()
        else:
            pl.when(condition)(run)

    def base(chunk):
        return 0 if every else chunk * members

    def is_member(chunk, device):
        return (device >= base(chunk)) & (device < base(chunk) + members)

    def window(ref, index):
        row = pl.multiple_of((index // col_groups) * rows, 16)
        if col_groups == 1:
            return ref.at[pl.ds(row, rows)]
        col = pl.multiple_of(lax.rem(index, col_groups) * width, LANES)
        return ref.at[pl.ds(row, rows), pl.ds(col, width)]

    chunks = ((mk_hbm, rx_k, st_k, mem_k), (mv_hbm, rx_v, st_v, mem_v))

    for c, (hbm, rx, st, mem) in enumerate(chunks):

        @pl.loop(1, n)
        def _(j):
            dest = lax.rem(me + j, n)

            def send():
                pltpu.make_async_remote_copy(
                    src_ref=window(hbm, dest - base(c)),
                    dst_ref=rx.at[me],
                    send_sem=p1_send.at[c],
                    recv_sem=p1_recv.at[c],
                    device_id={"dp": dest},
                    device_id_type=MESH,
                ).start()

            guard(is_member(c, dest), send)

        def own():
            pltpu.make_async_copy(
                window(hbm, me - base(c)), rx.at[me], p1_recv.at[c]
            ).start()

        guard(is_member(c, me), own)

    @pl.loop(0, n)
    def _(s):
        src_sm[s] = lax.fori_loop(
            0, n, lambda i, a: jnp.where(owner_ref[i] == s, i, a), jnp.int32(0)
        )

    kept_here = lax.fori_loop(
        0, n, lambda i, a: a + jnp.where(owner_ref[i] == me, kept_ref[i], 0), jnp.int32(0)
    )

    ki = lax.broadcasted_iota(jnp.int32, (pos_len, pos_len), 0)
    di = lax.broadcasted_iota(jnp.int32, (pos_len, pos_len), 1)
    total = ki + di
    flip = ((total == mem_len) | (total == mem_len + pos_len)).astype(jnp.float32)
    bias_pad = jnp.concatenate(
        [bias_ref[...], jnp.zeros((8 - heads, pos_len), jnp.float32)], axis=0
    )
    bias_rev = jnp.dot(bias_pad, flip, precision=HIGHEST, preferred_element_type=jnp.float32)

    qi = lax.broadcasted_iota(jnp.int32, (seg_len, seg_len), 0)
    ti = lax.broadcasted_iota(jnp.int32, (seg_len, seg_len), 1)
    causal = ti <= qi
    NT = (((1,), (1,)), ((), ()))
    TN = (((0,), (0,)), ((), ()))

    def cs(h):
        return slice(h * DH, (h + 1) * DH)

    def seg_scores(h):
        table = pltpu.roll(
            jnp.broadcast_to(bias_rev[h : h + 1], (seg_len, pos_len)),
            0,
            1,
            stride=1,
            stride_axis=0,
        )
        s = lax.dot_general(
            q_ref[:, cs(h)], k_ref[:, cs(h)], NT, preferred_element_type=jnp.float32
        )
        s = s * scale + table[:, mem_len:]
        prob[h, :, mem_len:] = jnp.where(causal, s, -1e30)
        prob[h, :, :mem_len] = table[:, :mem_len]

    def wait_first_and_forward(c):
        _, rx, st, mem = chunks[c]

        def run():
            pltpu.make_async_copy(rx, rx, p1_recv.at[c]).wait()

            @pl.loop(0, n)
            def _(s):
                st[s] = rx[src_sm[s]]

            @pl.loop(1, n)
            def _(j):
                dest = lax.rem(me + j, n)
                pltpu.make_async_remote_copy(
                    src_ref=st.at[dest],
                    dst_ref=window(mem, me - base(c)),
                    send_sem=p2_send.at[c],
                    recv_sem=p2_recv.at[c],
                    device_id={"dp": dest},
                    device_id_type=MESH,
                ).start()

            pltpu.make_async_copy(
                st.at[me], window(mem, me - base(c)), p2_recv.at[c]
            ).start()

        guard(is_member(c, me), run)

    for h in range(heads):
        seg_scores(h)
    wait_first_and_forward(0)
    wait_first_and_forward(1)
    pltpu.make_async_copy(mem_k, mem_k, p2_recv.at[0]).wait()

    mi = lax.broadcasted_iota(jnp.int32, (seg_len, mem_len), 1)
    live = mi >= mem_len - BLOCK * kept_here
    for h in range(heads):
        s_mem = lax.dot_general(
            q_ref[:, cs(h)], mem_k[:, cs(h)], NT, preferred_element_type=jnp.float32
        )
        s_mem = jnp.where(live, s_mem * scale + prob[h, :, :mem_len], -1e30)
        s_seg = prob[h, :, mem_len:]
        row_max = jnp.maximum(
            jnp.max(s_mem, axis=1, keepdims=True), jnp.max(s_seg, axis=1, keepdims=True)
        )
        e_mem = jnp.where(live, jnp.exp(s_mem - row_max), 0.0)
        e_seg = jnp.where(causal, jnp.exp(s_seg - row_max), 0.0)
        norm = 1.0 / (
            jnp.sum(e_mem, axis=1, keepdims=True) + jnp.sum(e_seg, axis=1, keepdims=True)
        )
        p_seg = e_seg * norm
        prob[h, :, :mem_len] = e_mem * norm
        prob[h, :, mem_len:] = p_seg
        attn[:, cs(h)] = jnp.dot(
            p_seg.astype(jnp.bfloat16), v_ref[:, cs(h)], preferred_element_type=jnp.float32
        )

    pltpu.make_async_copy(mem_v, mem_v, p2_recv.at[1]).wait()

    squares = jnp.zeros((seg_len, DH), jnp.float32)
    crosses = jnp.zeros((seg_len, DH), jnp.float32)
    for h in range(heads):
        out = attn[:, cs(h)] + jnp.dot(
            prob[h, :, :mem_len].astype(jnp.bfloat16),
            mem_v[:, cs(h)],
            preferred_element_type=jnp.float32,
        )
        attn[:, cs(h)] = out
        squares = squares + out * out
        crosses = crosses + cot_ref[:, cs(h)].astype(jnp.float32) * gain_ref[:, cs(h)] * out
    lane = lax.broadcasted_iota(jnp.int32, (seg_len, DH), 1)
    both = jnp.where(
        lane == 0,
        jnp.sum(squares, axis=1, keepdims=True),
        jnp.sum(crosses, axis=1, keepdims=True),
    )
    mp_send[...] = jnp.transpose(both)[:8]

    @pl.loop(1, n_mp)
    def _(j):
        pltpu.make_async_remote_copy(
            src_ref=mp_send,
            dst_ref=mp_recv.at[me_mp],
            send_sem=mp_ssem,
            recv_sem=mp_rsem,
            device_id={"mp": lax.rem(me_mp + j, n_mp)},
            device_id_type=MESH,
        ).start()

    pltpu.make_async_copy(mp_send, mp_recv.at[me_mp], mp_rsem).start()
    pltpu.make_async_copy(mp_recv, mp_recv, mp_rsem).wait()
    sums = mp_recv[0]
    for m in range(1, n_mp):
        sums = sums + mp_recv[m]
    sums = jnp.transpose(
        jnp.concatenate([sums, jnp.zeros((LANES - 8, seg_len), jnp.float32)], axis=0)
    )
    inv_rms = lax.rsqrt(sums[:, 0:1] / HD + 1e-06)
    pull = inv_rms * inv_rms * inv_rms * sums[:, 1:2] / HD

    gain_rows = []
    for h in range(heads):
        out = attn[:, cs(h)]
        gain = gain_ref[:, cs(h)]
        up = cot_ref[:, cs(h)].astype(jnp.float32)
        normed = out * inv_rms
        att_ref[:, cs(h)] = (normed * gain).astype(jnp.bfloat16)
        gain_rows.append(jnp.sum(up * normed, axis=0, keepdims=True))
        og = (inv_rms * (up * gain) - out * pull).astype(jnp.bfloat16)
        delta = jnp.sum(og.astype(jnp.float32) * out, axis=1, keepdims=True)
        p_mem = prob[h, :, :mem_len]
        p_seg = prob[h, :, mem_len:]
        g_mem = p_mem * (
            lax.dot_general(og, mem_v[:, cs(h)], NT, preferred_element_type=jnp.float32) - delta
        )
        g_seg = p_seg * (
            lax.dot_general(og, v_ref[:, cs(h)], NT, preferred_element_type=jnp.float32) - delta
        )
        gb_mem = g_mem.astype(jnp.bfloat16)
        gb_seg = g_seg.astype(jnp.bfloat16)
        dq = jnp.dot(gb_mem, mem_k[:, cs(h)], preferred_element_type=jnp.float32) + jnp.dot(
            gb_seg, k_ref[:, cs(h)], preferred_element_type=jnp.float32
        )
        dq_ref[:, cs(h)] = (dq * scale).astype(jnp.bfloat16)
        dk = lax.dot_general(gb_seg, q_ref[:, cs(h)], TN, preferred_element_type=jnp.float32)
        dk_ref[:, cs(h)] = (dk * scale).astype(jnp.bfloat16)
        dv = lax.dot_general(
            p_seg.astype(jnp.bfloat16), og, TN, preferred_element_type=jnp.float32
        )
        dv_ref[:, cs(h)] = dv.astype(jnp.bfloat16)
        x = jnp.concatenate([g_mem, g_seg], axis=1)
        half = seg_len // 2
        while half >= 8:
            x = x[:half] + pltpu.roll(x[half:], pos_len - half, 1)
            half //= 2
        folded[h * 8 : (h + 1) * 8] = x

    x = folded[...]
    for half in (4, 2, 1):
        x = x + pltpu.roll(pltpu.roll(x, pos_len - half, 1), heads * 8 - half, 0)
    rows8 = [x[8 * h : 8 * h + 1] for h in range(heads)]
    rows8.append(jnp.zeros((8 - heads, pos_len), jnp.float32))
    diag[...] = jnp.dot(
        jnp.concatenate(rows8, axis=0), flip, precision=HIGHEST, preferred_element_type=jnp.float32
    )
    gain_block = jnp.concatenate(
        gain_rows + [jnp.zeros((8 - heads, DH), jnp.float32)], axis=0
    )
    for b in range(pos_len // LANES):
        pkt[b, :8] = diag[:, b * LANES : (b + 1) * LANES]
        pkt[b, 8:] = gain_block

    part = pos_len // n

    @pl.loop(1, n)
    def _(j):
        dest = lax.rem(me + j, n)
        pltpu.make_async_remote_copy(
            src_ref=pkt.at[(dest * part) // LANES],
            dst_ref=pkt_recv.at[me],
            send_sem=dp_ssem,
            recv_sem=dp_rsem,
            device_id={"dp": dest},
            device_id_type=MESH,
        ).start()

    pltpu.make_async_copy(pkt.at[(me * part) // LANES], pkt_recv.at[me], dp_rsem).start()

    for c, (hbm, rx, st, mem) in enumerate(chunks):

        def wait_p1(count):
            pltpu.make_async_copy(
                rx.at[pl.ds(0, count)], rx.at[pl.ds(0, count)], p1_send.at[c]
            ).wait()

        def wait_p2():
            pltpu.make_async_copy(
                st.at[pl.ds(0, n - 1)], st.at[pl.ds(0, n - 1)], p2_send.at[c]
            ).wait()

        guard(is_member(c, me), functools.partial(wait_p1, members - 1))
        if not every:
            pl.when(jnp.logical_not(is_member(c, me)))(functools.partial(wait_p1, members))
        guard(is_member(c, me), wait_p2)
    pltpu.make_async_copy(
        mp_recv.at[pl.ds(0, n_mp - 1)], mp_recv.at[pl.ds(0, n_mp - 1)], mp_ssem
    ).wait()

    pltpu.make_async_copy(pkt_recv, pkt_recv, dp_rsem).wait()
    acc = pkt_recv[0]
    for s in range(1, n):
        acc = acc + pkt_recv[s]
    offset = lax.rem(me * part, LANES)
    mine = pltpu.roll(acc[:8], lax.rem(LANES - offset, LANES), 1)
    dbias_ref[...] = mine[:heads, :part]
    for h in range(heads):
        dgain_ref[:, cs(h)] = acc[8 + h : 9 + h]
    pltpu.make_async_copy(
        pkt_recv.at[pl.ds(0, n - 1)], pkt_recv.at[pl.ds(0, n - 1)], dp_ssem
    ).wait()


def body(
    n,
    n_mp,
    seg_queries,
    seg_keys,
    seg_values,
    memory_keys,
    memory_values,
    new_owner,
    kept_blocks,
    rel_bias,
    norm_gain,
    cotangent,
):
    _, seg_len, cols = seg_queries.shape
    mem_len = memory_keys.shape[1]
    heads, pos_len = rel_bias.shape
    part = pos_len // n
    plan = share_plan(n, mem_len, cols)
    members, rows, width, _ = plan
    bf16, f32 = jnp.bfloat16, jnp.float32
    vmem = pl.BlockSpec(memory_space=pltpu.VMEM)
    smem = pl.BlockSpec(memory_space=pltpu.SMEM)
    hbm = pl.BlockSpec(memory_space=pl.ANY)
    big = jax.ShapeDtypeStruct((seg_len, cols), bf16)
    outs = pl.pallas_call(
        functools.partial(kernel, n, n_mp, plan),
        out_shape=(
            big,
            big,
            big,
            big,
            jax.ShapeDtypeStruct((heads, part), f32),
            jax.ShapeDtypeStruct((1, cols), f32),
        ),
        in_specs=[smem, smem, vmem, vmem, vmem, hbm, hbm, vmem, vmem, vmem],
        out_specs=(vmem,) * 6,
        scratch_shapes=[
            pltpu.VMEM((n, rows, width), bf16),
            pltpu.VMEM((n, rows, width), bf16),
            pltpu.VMEM((n, rows, width), bf16),
            pltpu.VMEM((n, rows, width), bf16),
            pltpu.VMEM((mem_len, cols), bf16),
            pltpu.VMEM((mem_len, cols), bf16),
            pltpu.SMEM((n,), jnp.int32),
            pltpu.VMEM((heads, seg_len, pos_len), f32),
            pltpu.VMEM((seg_len, cols), f32),
            pltpu.VMEM((8, seg_len), f32),
            pltpu.VMEM((n_mp, 8, seg_len), f32),
            pltpu.VMEM((heads * 8, pos_len), f32),
            pltpu.VMEM((8, pos_len), f32),
            pltpu.VMEM((pos_len // LANES, 16, LANES), f32),
            pltpu.VMEM((n, 16, LANES), f32),
            pltpu.SemaphoreType.DMA((2,)),
            pltpu.SemaphoreType.DMA((2,)),
            pltpu.SemaphoreType.DMA((2,)),
            pltpu.SemaphoreType.DMA((2,)),
            pltpu.SemaphoreType.DMA,
            pltpu.SemaphoreType.DMA,
            pltpu.SemaphoreType.DMA,
            pltpu.SemaphoreType.DMA,
        ],
        compiler_params=pltpu.CompilerParams(
            collective_id=0, has_side_effects=True, vmem_limit_bytes=40 * 1024 * 1024
        ),
    )(
        new_owner,
        kept_blocks,
        seg_queries[0],
        seg_keys[0],
        seg_values[0],
        memory_keys[0],
        memory_values[0],
        rel_bias,
        norm_gain[None],
        cotangent[0],
    )
    return (
        outs[0][None],
        outs[1][None],
        outs[2][None],
        outs[3][None],
        outs[4],
        outs[5][0],
    )


def solution(mesh):
    rows = P("dp", None, "mp")
    in_specs = (rows, rows, rows, rows, rows, P(), P(), P("mp", None), P("mp"), rows)
    out_specs = (rows, rows, rows, rows, P("mp", "dp"), P("mp"))
    return jax.shard_map(
        functools.partial(body, mesh.shape["dp"], mesh.shape["mp"]),
        mesh=mesh,
        in_specs=in_specs,
        out_specs=out_specs,
        check_vma=False,
    )
```

time: 282 us -> 66 us (0.23); the launches traced: 278 us -> 65.6 us
  local copies, waits for them, and re-layouts: 116 us -> 10.9 us
  waiting for transfers between devices: 54.7 us -> 0 us
  Pallas kernels: 0 us -> 53.4 us
  blocking collectives: 50.3 us -> 0 us
  other arithmetic: 17.7 us -> 0.61 us
  starting transfers between devices: 15.2 us -> 0 us
  between operations: 15 us -> 0.66 us
  matrix products: 9.88 us -> 0 us
    pallas_call x0 -> x1, Pallas kernels: none -> 53.4 us  [body(): pl.pallas_call(functools.partial(kernel, n, n_mp, plan), out_shape=(big,...]
    rev x2 -> x0, local copies, waits for them, and re-layouts: 44.7 us -> none  [the longest x1 22.3 us: spread_table(): return skewed[:, ::-1, ::-1]]
    unnamed x2 -> x0, waiting for transfers between devices: 36.5 us -> none
    psum x3 -> x0, blocking collectives: 35.3 us -> none  [the longest x1 22.1 us: body(): gain_grad = lax.psum(local_gain, 'dp')]
    unnamed x60 -> x23, local copies, waits for them, and re-layouts: 29.3 us -> 10.2 us
    all_to_all x3 -> x0, waiting for transfers between devices: 18.2 us -> none  [the longest x1 11 us: body(): lax.all_to_all(memory_keys, 'dp', split_axis=1, concat_axis=0, tiled=True)]
    all_to_all x3 -> x0, starting transfers between devices: 15 us -> none  [the longest x1 7.28 us: body(): lax.all_to_all(memory_values, 'dp', split_axis=1, concat_axis=0, tiled=True)]
    all_to_all x1 -> x0, blocking collectives: 14.9 us -> none  [body(): lax.all_to_all(ordered[0], 'dp', split_axis=0, concat_axis=1, tiled=True)]
  transfers between devices with their start and end apart: 4 -> 0, of which waited for: 3 -> 0; matrix products, arithmetic and copies ran while one was open for 22% -> 0% of each run, Pallas kernels for 0% -> 0%
where the time goes in v1:
time: 66 us; the launch traced here: 65.6 us
  Pallas kernels  53.4 us (81%)
  local copies, waits for them, and re-layouts  10.9 us (17%)
  between operations  0.66 us (1%)
    pallas_call x1, Pallas kernels, body(): pl.pallas_call(functools.partial(kernel, n, n_mp, plan), out_shape=(big,...  53.4 us
    unnamed x23, local copies, waits for them, and re-layouts  10.2 us

profile of v1, /device:TPU:0, one launch (start us, length us, event | category | flops | bytes accessed | tf_op | source)
XLA Modules:
  0.0 65.6 jit_solution(1490796193065885966)
XLA Ops:
  0.6 0.0 copy-start.6
  0.6 0.7 %broadcast_in_dim.15.gain_ref = f32[1,768]{1,0:T(1,128)S(1)} reshape(f32[768]{0:T(1024)} %param.18) | data formatting | bytes 6144 | tf_op jit(solution)/shard_map/broadcast_in_dim | solution.py:462
  1.3 0.0 copy-start.7
  1.3 0.0 copy-start.8
  1.3 0.0 copy-done.6
  1.4 0.6 copy-done.7
  2.0 0.0 copy-done.8
  2.0 0.0 copy-start
  2.0 1.0 %copy-done = bf16[1,256,768]{2,1,0:T(8,128)(2,1)S(1)} copy-done((bf16[1,256,768]{2,1,0:T(8,128)(2,1)S(1)}, bf16[1,256,768]{2,1,0:T(8,128)(2,1)}, u32[]{:S(2)}) %copy-start) | copy-done | bytes 393240
  3.0 0.0 copy-start.1
  3.0 1.0 %copy-done.1 = bf16[1,256,768]{2,1,0:T(8,128)(2,1)S(1)} copy-done((bf16[1,256,768]{2,1,0:T(8,128)(2,1)S(1)}, bf16[1,256,768]{2,1,0:T(8,128)(2,1)}, u32[]{:S(2)}) %copy-start.1) | copy-done | bytes 393240
  4.0 0.0 copy-start.2
  4.0 1.0 %copy-done.2 = bf16[1,256,768]{2,1,0:T(8,128)(2,1)S(1)} copy-done((bf16[1,256,768]{2,1,0:T(8,128)(2,1)S(1)}, bf16[1,256,768]{2,1,0:T(8,128)(2,1)}, u32[]{:S(2)}) %copy-start.2) | copy-done | bytes 393240
  5.0 0.0 copy-start.3
  5.0 1.0 %copy-done.3 = bf16[1,256,768]{2,1,0:T(8,128)(2,1)S(1)} copy-done((bf16[1,256,768]{2,1,0:T(8,128)(2,1)S(1)}, bf16[1,256,768]{2,1,0:T(8,128)(2,1)}, u32[]{:S(2)}) %copy-start.3) | copy-done | bytes 393240
  6.0 0.0 copy-start.4
  6.0 1.0 %copy-done.4 = bf16[1,256,768]{2,1,0:T(8,128)(2,1)S(1)} copy-done((bf16[1,256,768]{2,1,0:T(8,128)(2,1)S(1)}, bf16[1,256,768]{2,1,0:T(8,128)(2,1)}, u32[]{:S(2)}) %copy-start.4) | copy-done | bytes 393240
  7.0 0.0 copy-start.5
  7.0 1.0 %copy-done.5 = bf16[1,256,768]{2,1,0:T(8,128)(2,1)S(1)} copy-done((bf16[1,256,768]{2,1,0:T(8,128)(2,1)S(1)}, bf16[1,256,768]{2,1,0:T(8,128)(2,1)}, u32[]{:S(2)}) %copy-start.5) | copy-done | bytes 393240
  8.0 53.4 %shard_map.145 = (bf16[256,768]{1,0:T(8,128)(2,1)S(1)}, bf16[256,768]{1,0:T(8,128)(2,1)S(1)}, bf16[256,768]{1,0:T(8,128)(2,1)S(1)}, bf16[256,768]{1,0:T(8,128)(2...) custom-call(s32[8]{0:T(128)S(1)} %copy-done.7, s32[8]{0:T(128)S(1)} %copy-done.8, bf16[256,768]{1,0:T(8,128)(2,1)S(1)} %bitcast.10, ...), custom_call_target="tpu_custom_call" | custom-call | tf_op jit(solution)/shard_map/pallas_call | solution.py:413
  61.4 0.6 reduce
  62.0 0.7 %copy.21 = bf16[1,256,768]{2,1,0:T(8,128)(2,1)} copy(bf16[1,256,768]{2,1,0:T(8,128)(2,1)S(1)} %bitcast.19) | data formatting | bytes 786432
  62.7 0.7 %copy.22 = bf16[1,256,768]{2,1,0:T(8,128)(2,1)} copy(bf16[1,256,768]{2,1,0:T(8,128)(2,1)S(1)} %bitcast.18) | data formatting | bytes 786432
  63.5 0.7 %copy.23 = bf16[1,256,768]{2,1,0:T(8,128)(2,1)} copy(bf16[1,256,768]{2,1,0:T(8,128)(2,1)S(1)} %bitcast.17) | data formatting | bytes 786432
  64.2 0.7 %copy.24 = bf16[1,256,768]{2,1,0:T(8,128)(2,1)} copy(bf16[1,256,768]{2,1,0:T(8,128)(2,1)S(1)} %bitcast.16) | data formatting | bytes 786432
  65.0 0.6 copy.25
Async XLA Ops:
  0.6 0.7 %copy-start.6 = (f32[6,512]{1,0:T(8,128)S(1)}, f32[6,512]{1,0:T(8,128)}, u32[]{:S(2)}) copy-start(f32[6,512]{1,0:T(8,128)} %bias_ref.1) | copy-start | bytes 36868
  1.3 0.7 %copy-start.7 = (s32[8]{0:T(128)S(1)}, s32[8]{0:T(128)}, u32[]{:S(2)}) copy-start(s32[8]{0:T(128)} %owner_ref.1) | copy-start | bytes 100
  1.3 0.7 %copy-start.8 = (s32[8]{0:T(128)S(1)}, s32[8]{0:T(128)}, u32[]{:S(2)}) copy-start(s32[8]{0:T(128)} %kept_ref.1) | copy-start | bytes 100
  2.0 1.0 %copy-start = (bf16[1,256,768]{2,1,0:T(8,128)(2,1)S(1)}, bf16[1,256,768]{2,1,0:T(8,128)(2,1)}, u32[]{:S(2)}) copy-start(bf16[1,256,768]{2,1,0:T(8,128)(2,1)} %param.10) | copy-start | bytes 1179652
  3.0 1.0 %copy-start.1 = (bf16[1,256,768]{2,1,0:T(8,128)(2,1)S(1)}, bf16[1,256,768]{2,1,0:T(8,128)(2,1)}, u32[]{:S(2)}) copy-start(bf16[1,256,768]{2,1,0:T(8,128)(2,1)} %param.11) | copy-start | bytes 1179652
  4.0 1.0 %copy-start.2 = (bf16[1,256,768]{2,1,0:T(8,128)(2,1)S(1)}, bf16[1,256,768]{2,1,0:T(8,128)(2,1)}, u32[]{:S(2)}) copy-start(bf16[1,256,768]{2,1,0:T(8,128)(2,1)} %param.12) | copy-start | bytes 1179652
  5.0 1.0 %copy-start.3 = (bf16[1,256,768]{2,1,0:T(8,128)(2,1)S(1)}, bf16[1,256,768]{2,1,0:T(8,128)(2,1)}, u32[]{:S(2)}) copy-start(bf16[1,256,768]{2,1,0:T(8,128)(2,1)} %param.13) | copy-start | bytes 1179652
  6.0 1.0 %copy-start.4 = (bf16[1,256,768]{2,1,0:T(8,128)(2,1)S(1)}, bf16[1,256,768]{2,1,0:T(8,128)(2,1)}, u32[]{:S(2)}) copy-start(bf16[1,256,768]{2,1,0:T(8,128)(2,1)} %param.14) | copy-start | bytes 1179652
  7.0 1.0 %copy-start.5 = (bf16[1,256,768]{2,1,0:T(8,128)(2,1)S(1)}, bf16[1,256,768]{2,1,0:T(8,128)(2,1)}, u32[]{:S(2)}) copy-start(bf16[1,256,768]{2,1,0:T(8,128)(2,1)} %param.19) | copy-start | bytes 1179652

commit v2 on v1

--- a/solution.py
+++ b/solution.py
@@ -30,20 +30,32 @@
     plan,
     owner_ref,
     kept_ref,
+    q_hbm,
+    k_hbm,
+    v_hbm,
+    mk_hbm,
+    mv_hbm,
+    bias_hbm,
+    gain_ref,
+    cot_hbm,
+    att_hbm,
+    dq_hbm,
+    dk_hbm,
+    dv_hbm,
+    dbias_ref,
+    dgain_ref,
     q_ref,
     k_ref,
     v_ref,
-    mk_hbm,
-    mv_hbm,
     bias_ref,
-    gain_ref,
     cot_ref,
     att_ref,
     dq_ref,
     dk_ref,
     dv_ref,
-    dbias_ref,
-    dgain_ref,
+    grads,
+    in_sem,
+    out_sem,
     rx_k,
     rx_v,
     st_k,
@@ -78,6 +90,18 @@
     scale = DH ** (-0.5)
     every = members == n
 
+    loads = [
+        pltpu.make_async_copy(a, b, in_sem.at[i])
+        for i, (a, b) in enumerate(
+            (
+                (bias_hbm, bias_ref),
+                (q_hbm, q_ref),
+                (k_hbm, k_ref),
+                (v_hbm, v_ref),
+                (cot_hbm, cot_ref),
+            )
+        )
+    ]
     barrier = pltpu.get_barrier_semaphore()
 
     @pl.loop(1, n)
@@ -140,6 +164,9 @@
 
         guard(is_member(c, me), own)
 
+    for load in loads:
+        load.start()
+
     @pl.loop(0, n)
     def _(s):
         src_sm[s] = lax.fori_loop(
@@ -150,6 +177,7 @@
         0, n, lambda i, a: a + jnp.where(owner_ref[i] == me, kept_ref[i], 0), jnp.int32(0)
     )
 
+    loads[0].wait()
     ki = lax.broadcasted_iota(jnp.int32, (pos_len, pos_len), 0)
     di = lax.broadcasted_iota(jnp.int32, (pos_len, pos_len), 1)
     total = ki + di
@@ -211,6 +239,8 @@
 
         guard(is_member(c, me), run)
 
+    for load in loads[1:]:
+        load.wait()
     for h in range(heads):
         seg_scores(h)
     wait_first_and_forward(0)
@@ -252,7 +282,7 @@
         )
         attn[:, cs(h)] = out
         squares = squares + out * out
-        crosses = crosses + cot_ref[:, cs(h)].astype(jnp.float32) * gain_ref[:, cs(h)] * out
+        crosses = crosses + cot_ref[:, cs(h)].astype(jnp.float32) * gain_ref[cs(h)][None] * out
     lane = lax.broadcasted_iota(jnp.int32, (seg_len, DH), 1)
     both = jnp.where(
         lane == 0,
@@ -283,10 +313,10 @@
     inv_rms = lax.rsqrt(sums[:, 0:1] / HD + 1e-06)
     pull = inv_rms * inv_rms * inv_rms * sums[:, 1:2] / HD
 
-    gain_rows = []
+    gain_rows, out_grads = [], []
     for h in range(heads):
         out = attn[:, cs(h)]
-        gain = gain_ref[:, cs(h)]
+        gain = gain_ref[cs(h)][None]
         up = cot_ref[:, cs(h)].astype(jnp.float32)
         normed = out * inv_rms
         att_ref[:, cs(h)] = (normed * gain).astype(jnp.bfloat16)
@@ -301,18 +331,9 @@
         g_seg = p_seg * (
             lax.dot_general(og, v_ref[:, cs(h)], NT, preferred_element_type=jnp.float32) - delta
         )
-        gb_mem = g_mem.astype(jnp.bfloat16)
-        gb_seg = g_seg.astype(jnp.bfloat16)
-        dq = jnp.dot(gb_mem, mem_k[:, cs(h)], preferred_element_type=jnp.float32) + jnp.dot(
-            gb_seg, k_ref[:, cs(h)], preferred_element_type=jnp.float32
-        )
-        dq_ref[:, cs(h)] = (dq * scale).astype(jnp.bfloat16)
-        dk = lax.dot_general(gb_seg, q_ref[:, cs(h)], TN, preferred_element_type=jnp.float32)
-        dk_ref[:, cs(h)] = (dk * scale).astype(jnp.bfloat16)
-        dv = lax.dot_general(
-            p_seg.astype(jnp.bfloat16), og, TN, preferred_element_type=jnp.float32
-        )
-        dv_ref[:, cs(h)] = dv.astype(jnp.bfloat16)
+        grads[h, :, :mem_len] = g_mem.astype(jnp.bfloat16)
+        grads[h, :, mem_len:] = g_seg.astype(jnp.bfloat16)
+        out_grads.append(og)
         x = jnp.concatenate([g_mem, g_seg], axis=1)
         half = seg_len // 2
         while half >= 8:
@@ -351,6 +372,35 @@
 
     pltpu.make_async_copy(pkt.at[(me * part) // LANES], pkt_recv.at[me], dp_rsem).start()
 
+    stores = [
+        pltpu.make_async_copy(a, b, out_sem.at[i])
+        for i, (a, b) in enumerate(
+            ((att_ref, att_hbm), (dv_ref, dv_hbm), (dk_ref, dk_hbm), (dq_ref, dq_hbm))
+        )
+    ]
+    stores[0].start()
+    for h in range(heads):
+        dv = lax.dot_general(
+            prob[h, :, mem_len:].astype(jnp.bfloat16),
+            out_grads[h],
+            TN,
+            preferred_element_type=jnp.float32,
+        )
+        dv_ref[:, cs(h)] = dv.astype(jnp.bfloat16)
+    stores[1].start()
+    for h in range(heads):
+        dk = lax.dot_general(
+            grads[h, :, mem_len:], q_ref[:, cs(h)], TN, preferred_element_type=jnp.float32
+        )
+        dk_ref[:, cs(h)] = (dk * scale).astype(jnp.bfloat16)
+    stores[2].start()
+    for h in range(heads):
+        dq = jnp.dot(
+            grads[h, :, :mem_len], mem_k[:, cs(h)], preferred_element_type=jnp.float32
+        ) + jnp.dot(grads[h, :, mem_len:], k_ref[:, cs(h)], preferred_element_type=jnp.float32)
+        dq_ref[:, cs(h)] = (dq * scale).astype(jnp.bfloat16)
+    stores[3].start()
+
     for c, (hbm, rx, st, mem) in enumerate(chunks):
 
         def wait_p1(count):
@@ -379,10 +429,24 @@
     mine = pltpu.roll(acc[:8], lax.rem(LANES - offset, LANES), 1)
     dbias_ref[...] = mine[:heads, :part]
     for h in range(heads):
-        dgain_ref[:, cs(h)] = acc[8 + h : 9 + h]
+        dgain_ref[cs(h)] = acc[8 + h]
+    for store in stores:
+        store.wait()
     pltpu.make_async_copy(
         pkt_recv.at[pl.ds(0, n - 1)], pkt_recv.at[pl.ds(0, n - 1)], dp_ssem
     ).wait()
+
+
+def hand_on(*refs):
+    count = len(refs) // 2
+    sem = refs[-1]
+    copies = [
+        pltpu.make_async_copy(refs[i], refs[count + i], sem.at[i]) for i in range(count)
+    ]
+    for copy in copies:
+        copy.start()
+    for copy in copies:
+        copy.wait()
 
 
 def body(
@@ -418,11 +482,23 @@
             big,
             big,
             jax.ShapeDtypeStruct((heads, part), f32),
-            jax.ShapeDtypeStruct((1, cols), f32),
+            jax.ShapeDtypeStruct((cols,), f32),
         ),
-        in_specs=[smem, smem, vmem, vmem, vmem, hbm, hbm, vmem, vmem, vmem],
-        out_specs=(vmem,) * 6,
+        in_specs=[smem, smem, hbm, hbm, hbm, hbm, hbm, hbm, vmem, hbm],
+        out_specs=(hbm,) * 4 + (vmem,) * 2,
         scratch_shapes=[
+            pltpu.VMEM((seg_len, cols), bf16),
+            pltpu.VMEM((seg_len, cols), bf16),
+            pltpu.VMEM((seg_len, cols), bf16),
+            pltpu.VMEM((heads, pos_len), f32),
+            pltpu.VMEM((seg_len, cols), bf16),
+            pltpu.VMEM((seg_len, cols), bf16),
+            pltpu.VMEM((seg_len, cols), bf16),
+            pltpu.VMEM((seg_len, cols), bf16),
+            pltpu.VMEM((seg_len, cols), bf16),
+            pltpu.VMEM((heads, seg_len, pos_len), bf16),
+            pltpu.SemaphoreType.DMA((5,)),
+            pltpu.SemaphoreType.DMA((4,)),
             pltpu.VMEM((n, rows, width), bf16),
             pltpu.VMEM((n, rows, width), bf16),
             pltpu.VMEM((n, rows, width), bf16),
@@ -448,7 +524,7 @@
             pltpu.SemaphoreType.DMA,
         ],
         compiler_params=pltpu.CompilerParams(
-            collective_id=0, has_side_effects=True, vmem_limit_bytes=40 * 1024 * 1024
+            collective_id=0, has_side_effects=True, vmem_limit_bytes=60 * 1024 * 1024
         ),
     )(
         new_owner,
@@ -459,16 +535,24 @@
         memory_keys[0],
         memory_values[0],
         rel_bias,
-        norm_gain[None],
+        norm_gain,
         cotangent[0],
     )
+    final = pl.pallas_call(
+        hand_on,
+        out_shape=tuple(jax.ShapeDtypeStruct(o.shape, o.dtype) for o in outs),
+        in_specs=[hbm] * 6,
+        out_specs=(hbm,) * 6,
+        scratch_shapes=[pltpu.SemaphoreType.DMA((6,))],
+        compiler_params=pltpu.CompilerParams(vmem_limit_bytes=60 * 1024 * 1024),
+    )(*outs)
     return (
-        outs[0][None],
-        outs[1][None],
-        outs[2][None],
-        outs[3][None],
-        outs[4],
-        outs[5][0],
+        final[0][None],
+        final[1][None],
+        final[2][None],
+        final[3][None],
+        final[4],
+        final[5],
     )
 
 

time: 66 us -> 103 us (1.56)
  Pallas kernels: 53.4 us -> 102 us
  local copies, waits for them, and re-layouts: 10.9 us -> 0 us
    pallas_call x0 -> x1, Pallas kernels: none -> 49 us  [body(): pl.pallas_call(hand_on, out_shape=tuple((jax.ShapeDtypeStruct(o.shape, o....]
    unnamed x23 -> x0, local copies, waits for them, and re-layouts: 10.2 us -> none
where the time goes in v2:
time: 103 us
  Pallas kernels  102 us (99%)
    pallas_call x1, Pallas kernels, body(): pl.pallas_call(functools.partial(kernel, n, n_mp, plan), out_shape=(big,...  53 us
    pallas_call x1, Pallas kernels, body(): pl.pallas_call(hand_on, out_shape=tuple((jax.ShapeDtypeStruct(o.shape, o....  49 us

profile of v2, /device:TPU:0, one launch (start us, length us, event | category | flops | bytes accessed | tf_op | source)
XLA Modules:
  0.0 102.6 jit_solution(10706731139936471282)
XLA Ops:
  0.6 53.0 %shard_map.145 = (bf16[256,768]{1,0:T(8,128)(2,1)}, bf16[256,768]{1,0:T(8,128)(2,1)}, bf16[256,768]{1,0:T(8,128)(2,1)}, bf16[256,768]{1,0:T(8,128)(2,1)}, f32[6,64]{1,0:T(8,128)}, /*index=5*/f32[768]{0:T(1024)}) custom-call(s32[8]{0:T(128)} %owner_ref.1, s32[8]{0:T(128)} %kept_ref.1, bf16[256,768]{1,0:T(8,128)(2,1)} %bitcast.10, bf16[256,768]{1,0:T(8,128)(2,1)} %bitcast.11, ...), custom_call_target="tpu_custom_call" | custom-call | tf_op jit(solution)/shard_map/pallas_call | solution.py:477
  53.6 49.0 %shard_map.146 = (bf16[256,768]{1,0:T(8,128)(2,1)}, bf16[256,768]{1,0:T(8,128)(2,1)}, bf16[256,768]{1,0:T(8,128)(2,1)}, bf16[256,768]{1,0:T(8,128)(2,1)}, f32[6,64]{1,0:T(8,128)}, /*index=5*/f32[768]{0:T(1024)}) custom-call(bf16[256,768]{1,0:T(8,128)(2,1)} %get-tuple-element.18.refs_0_, bf16[256,768]{1,0:T(8,128)(2,1)} %get-tuple-element.19.refs_1_, ...), custom_call_target="tpu_custom_call" | custom-call | tf_op jit(solution)/shard_map/pallas_call | solution.py:541

commit v3 on v2

--- a/solution.py
+++ b/solution.py
@@ -28,15 +28,15 @@
     n,
     n_mp,
     plan,
-    owner_ref,
-    kept_ref,
+    owner_hbm,
+    kept_hbm,
     q_hbm,
     k_hbm,
     v_hbm,
     mk_hbm,
     mv_hbm,
     bias_hbm,
-    gain_ref,
+    gain_hbm,
     cot_hbm,
     att_hbm,
     dq_hbm,
@@ -49,6 +49,9 @@
     v_ref,
     bias_ref,
     cot_ref,
+    gain_ref,
+    owner_ref,
+    kept_ref,
     att_ref,
     dq_ref,
     dk_ref,
@@ -94,7 +97,10 @@
         pltpu.make_async_copy(a, b, in_sem.at[i])
         for i, (a, b) in enumerate(
             (
+                (owner_hbm, owner_ref),
+                (kept_hbm, kept_ref),
                 (bias_hbm, bias_ref),
+                (gain_hbm, gain_ref),
                 (q_hbm, q_ref),
                 (k_hbm, k_ref),
                 (v_hbm, v_ref),
@@ -102,6 +108,8 @@
             )
         )
     ]
+    for load in loads:
+        load.start()
     barrier = pltpu.get_barrier_semaphore()
 
     @pl.loop(1, n)
@@ -117,6 +125,18 @@
         )
 
     pl.semaphore_wait(barrier, n - 1 + n_mp - 1)
+
+    near = n // 2
+    side = me // near
+
+    def each_peer(run):
+        @pl.loop(0, near)
+        def _(i):
+            run((1 - side) * near + lax.rem(me + i, near))
+
+        @pl.loop(1, near)
+        def _(i):
+            run(side * near + lax.rem(me + i, near))
 
     def guard(condition, run):
         if every:
@@ -141,10 +161,7 @@
 
     for c, (hbm, rx, st, mem) in enumerate(chunks):
 
-        @pl.loop(1, n)
-        def _(j):
-            dest = lax.rem(me + j, n)
-
+        def first(dest):
             def send():
                 pltpu.make_async_remote_copy(
                     src_ref=window(hbm, dest - base(c)),
@@ -157,6 +174,8 @@
 
             guard(is_member(c, dest), send)
 
+        each_peer(first)
+
         def own():
             pltpu.make_async_copy(
                 window(hbm, me - base(c)), rx.at[me], p1_recv.at[c]
@@ -164,9 +183,8 @@
 
         guard(is_member(c, me), own)
 
-    for load in loads:
-        load.start()
-
+    loads[0].wait()
+    loads[1].wait()
     @pl.loop(0, n)
     def _(s):
         src_sm[s] = lax.fori_loop(
@@ -177,7 +195,7 @@
         0, n, lambda i, a: a + jnp.where(owner_ref[i] == me, kept_ref[i], 0), jnp.int32(0)
     )
 
-    loads[0].wait()
+    loads[2].wait()
     ki = lax.broadcasted_iota(jnp.int32, (pos_len, pos_len), 0)
     di = lax.broadcasted_iota(jnp.int32, (pos_len, pos_len), 1)
     total = ki + di
@@ -221,9 +239,7 @@
             def _(s):
                 st[s] = rx[src_sm[s]]
 
-            @pl.loop(1, n)
-            def _(j):
-                dest = lax.rem(me + j, n)
+            def second(dest):
                 pltpu.make_async_remote_copy(
                     src_ref=st.at[dest],
                     dst_ref=window(mem, me - base(c)),
@@ -233,13 +249,14 @@
                     device_id_type=MESH,
                 ).start()
 
+            each_peer(second)
             pltpu.make_async_copy(
                 st.at[me], window(mem, me - base(c)), p2_recv.at[c]
             ).start()
 
         guard(is_member(c, me), run)
 
-    for load in loads[1:]:
+    for load in loads[3:]:
         load.wait()
     for h in range(heads):
         seg_scores(h)
@@ -358,9 +375,7 @@
 
     part = pos_len // n
 
-    @pl.loop(1, n)
-    def _(j):
-        dest = lax.rem(me + j, n)
+    def packet(dest):
         pltpu.make_async_remote_copy(
             src_ref=pkt.at[(dest * part) // LANES],
             dst_ref=pkt_recv.at[me],
@@ -370,6 +385,7 @@
             device_id_type=MESH,
         ).start()
 
+    each_peer(packet)
     pltpu.make_async_copy(pkt.at[(me * part) // LANES], pkt_recv.at[me], dp_rsem).start()
 
     stores = [
@@ -438,15 +454,22 @@
 
 
 def hand_on(*refs):
-    count = len(refs) // 2
-    sem = refs[-1]
-    copies = [
-        pltpu.make_async_copy(refs[i], refs[count + i], sem.at[i]) for i in range(count)
+    count = (len(refs) - 2) // 3
+    given, taken, held = refs[:count], refs[count : 2 * count], refs[2 * count : 3 * count]
+    in_sem, out_sem = refs[-2:]
+    loads = [
+        pltpu.make_async_copy(given[i], held[i], in_sem.at[i]) for i in range(count)
     ]
-    for copy in copies:
-        copy.start()
-    for copy in copies:
-        copy.wait()
+    stores = [
+        pltpu.make_async_copy(held[i], taken[i], out_sem.at[i]) for i in range(count)
+    ]
+    for load in loads:
+        load.start()
+    for load, store in zip(loads, stores):
+        load.wait()
+        store.start()
+    for store in stores:
+        store.wait()
 
 
 def body(
@@ -471,8 +494,7 @@
     members, rows, width, _ = plan
     bf16, f32 = jnp.bfloat16, jnp.float32
     vmem = pl.BlockSpec(memory_space=pltpu.VMEM)
-    smem = pl.BlockSpec(memory_space=pltpu.SMEM)
-    hbm = pl.BlockSpec(memory_space=pl.ANY)
+    hbm = pl.BlockSpec(memory_space=pltpu.HBM)
     big = jax.ShapeDtypeStruct((seg_len, cols), bf16)
     outs = pl.pallas_call(
         functools.partial(kernel, n, n_mp, plan),
@@ -484,7 +506,7 @@
             jax.ShapeDtypeStruct((heads, part), f32),
             jax.ShapeDtypeStruct((cols,), f32),
         ),
-        in_specs=[smem, smem, hbm, hbm, hbm, hbm, hbm, hbm, vmem, hbm],
+        in_specs=[hbm] * 10,
         out_specs=(hbm,) * 4 + (vmem,) * 2,
         scratch_shapes=[
             pltpu.VMEM((seg_len, cols), bf16),
@@ -492,12 +514,15 @@
             pltpu.VMEM((seg_len, cols), bf16),
             pltpu.VMEM((heads, pos_len), f32),
             pltpu.VMEM((seg_len, cols), bf16),
+            pltpu.VMEM((cols,), f32),
+            pltpu.SMEM((n,), jnp.int32),
+            pltpu.SMEM((n,), jnp.int32),
             pltpu.VMEM((seg_len, cols), bf16),
             pltpu.VMEM((seg_len, cols), bf16),
             pltpu.VMEM((seg_len, cols), bf16),
             pltpu.VMEM((seg_len, cols), bf16),
             pltpu.VMEM((heads, seg_len, pos_len), bf16),
-            pltpu.SemaphoreType.DMA((5,)),
+            pltpu.SemaphoreType.DMA((9,)),
             pltpu.SemaphoreType.DMA((4,)),
             pltpu.VMEM((n, rows, width), bf16),
             pltpu.VMEM((n, rows, width), bf16),
@@ -543,7 +568,8 @@
         out_shape=tuple(jax.ShapeDtypeStruct(o.shape, o.dtype) for o in outs),
         in_specs=[hbm] * 6,
         out_specs=(hbm,) * 6,
-        scratch_shapes=[pltpu.SemaphoreType.DMA((6,))],
+        scratch_shapes=[pltpu.VMEM(o.shape, o.dtype) for o in outs]
+        + [pltpu.SemaphoreType.DMA((6,)), pltpu.SemaphoreType.DMA((6,))],
         compiler_params=pltpu.CompilerParams(vmem_limit_bytes=60 * 1024 * 1024),
     )(*outs)
     return (

time: 103 us -> 55 us (0.53)
  Pallas kernels: 102 us -> 54.2 us
    pallas_call x1, Pallas kernels: 49 us -> 2.24 us  [body(): pl.pallas_call(hand_on, out_shape=tuple((jax.ShapeDtypeStruct(o.shape, o....]
where the time goes in v3:
time: 55 us; the launch traced here: 54.9 us
  Pallas kernels  54.2 us (99%)
  between operations  0.64 us (1%)
    pallas_call x1, Pallas kernels, body(): pl.pallas_call(functools.partial(kernel, n, n_mp, plan), out_shape=(big,...  52 us
    pallas_call x1, Pallas kernels, body(): pl.pallas_call(hand_on, out_shape=tuple((jax.ShapeDtypeStruct(o.shape, o....  2.24 us

profile of v3, /device:TPU:0, one launch (start us, length us, event | category | flops | bytes accessed | tf_op | source)
XLA Modules:
  0.0 54.9 jit_solution(164917054764755744)
XLA Ops:
  0.6 52.0 %shard_map.145 = (bf16[256,768]{1,0:T(8,128)(2,1)}, bf16[256,768]{1,0:T(8,128)(2,1)}, bf16[256,768]{1,0:T(8,128)(2,1)}, bf16[256,768]{1,0:T(8,128)(2,1)}, f32[6,64]{1,0:T(8,128)}, /*index=5*/f32[768]{0:T(1024)}) custom-call(s32[8]{0:T(128)} %owner_hbm.1, s32[8]{0:T(128)} %kept_hbm.1, bf16[256,768]{1,0:T(8,128)(2,1)} %bitcast.10, bf16[256,768]{1,0:T(8,128)(2,1)} %bitcast.11, ...), custom_call_target="tpu_custom_call" | custom-call | tf_op jit(solution)/shard_map/pallas_call | solution.py:499
  52.7 2.2 %shard_map.146 = (bf16[256,768]{1,0:T(8,128)(2,1)}, bf16[256,768]{1,0:T(8,128)(2,1)}, bf16[256,768]{1,0:T(8,128)(2,1)}, bf16[256,768]{1,0:T(8,128)(2,1)}, f32[6,64]{1,0:T(8,128)}, /*index=5*/f32[768]{0:T(1024)}) custom-call(bf16[256,768]{1,0:T(8,128)(2,1)} %get-tuple-element.18.refs_0_, bf16[256,768]{1,0:T(8,128)(2,1)} %get-tuple-element.19.refs_1_, ...), custom_call_target="tpu_custom_call" | custom-call | tf_op jit(solution)/shard_map/pallas_call | solution.py:566
